TPU v7x, 32 devices: a whole 2x2x4 slice. The times are simulated.
32 devices in a mesh: groups: 2 (over y), row: 4 (over z), col: 4 (over x, core).
Axes of the slice: x: 2, y: 2, z: 4, core: 2. Of those that a mesh axis runs over, the one named last changes fastest.
Arguments:
- features: bfloat16 [8, 2048, 256], P(('groups', 'row'), 'col'), parts along dimension 0, may hold values from -6 to 6
- tile_values: bfloat16 [8, 4, 1024, 4096], P(('groups', 'row'), 'col'), parts along dimension 0, may hold values from -0.125 to 0.125
- tile_rows: int32 [8, 4, 1024], P(('groups', 'row'), 'col'), parts along dimension 0, may hold values from 0 to 31
- tile_cols: int32 [8, 4, 1024], P(('groups', 'row'), 'col'), parts along dimension 0, may hold values from 0 to 31
- counts: int32 [8, 4], P(('groups', 'row'), 'col'), parts along dimension 0, may hold values from 128 to 1024, as said below
- weight: bfloat16 [256, 256], replicated, may hold values from -0.375 to 0.375
- bias: float32 [256], replicated, may hold values from -3 to 3
Outputs:
- layer_out: bfloat16 [8, 2048, 256], P(('groups', 'col'), 'row'), parts along dimension 0
There are 2 independent parts, one for each index of `groups`. A program takes and returns all parts, laid end to end along the dimension named above; an argument that names none is the same for every part. Nothing has to cross between parts.
Inputs may be any that keep to these rules, and one draw needn't show every extreme that they name: Slots at or past counts[r, c] hold values that are to be ignored; coordinate pairs may repeat within a cell, and repeated tiles add. In every draw one grid cell has exactly 1024 live slots.
All inputs are finite; a program needn't handle non-finite values.
Results may differ from a plain program's by a relative error of at most 0.0046.
Values may be sent and summed in bfloat16 or wider, within the bound.
A program may use at most 128 MiB of HBM per device.

v0:
```python
import jax
import jax.numpy as jnp
from jax import lax
from jax.sharding import PartitionSpec as P

TILE = 64


def on_device(features, tile_values, tile_rows, tile_cols, counts, weight, bias):
    piece_rows = features.shape[1]
    feat_width = features.shape[2]
    gathered = lax.all_gather(features, "col", axis=1, tiled=True)
    source = gathered.reshape(-1, TILE, feat_width)
    slot_count = tile_values.shape[2]
    block_size = min(128, slot_count)
    out_tiles = lax.axis_size("row") * piece_rows // TILE
    values = tile_values.reshape(slot_count, TILE, TILE)
    tile_row = tile_rows.reshape(slot_count)
    tile_col = tile_cols.reshape(slot_count)
    live_count = counts.reshape(())
    tile_ids = jnp.arange(out_tiles, dtype=jnp.int32)

    def block_step(block_index, running):
        first_slot = block_index * block_size
        tile_block = lax.dynamic_slice_in_dim(values, first_slot, block_size, 0)
        target_rows = lax.dynamic_slice_in_dim(tile_row, first_slot, block_size, 0)
        source_cols = lax.dynamic_slice_in_dim(tile_col, first_slot, block_size, 0)
        inputs = source[source_cols]
        products = jnp.einsum(
            "bij,bjf->bif", tile_block, inputs, preferred_element_type=jnp.float32
        )
        is_live = first_slot + jnp.arange(block_size, dtype=jnp.int32) < live_count
        target = jnp.where(is_live, target_rows, out_tiles)
        selector = (tile_ids[:, None] == target[None, :]).astype(jnp.float32)
        flat_products = products.reshape(block_size, TILE * feat_width)
        added = jnp.dot(
            selector,
            flat_products,
            precision=lax.Precision.HIGHEST,
            preferred_element_type=jnp.float32,
        )
        return running + added

    running = jnp.zeros((out_tiles, TILE * feat_width), jnp.float32)
    block_count = slot_count // block_size
    running = lax.fori_loop(0, block_count, block_step, running)
    partial_value = running.reshape(-1, feat_width)
    own_rows = lax.psum_scatter(partial_value, "row", scatter_dimension=0, tiled=True)
    hidden = own_rows.astype(jnp.bfloat16)
    mixed = jnp.dot(hidden, weight, preferred_element_type=jnp.float32) + bias
    return jnp.maximum(mixed, 0.0).astype(jnp.bfloat16).reshape(1, piece_rows, feat_width)


def solution(mesh):
    in_specs = (
        P(("groups", "row"), "col", None),
        P(("groups", "row"), "col", None, None),
        P(("groups", "row"), "col", None),
        P(("groups", "row"), "col", None),
        P(("groups", "row"), "col"),
        P(),
        P(),
    )
    out_specs = P(("groups", "col"), "row", None)
    return jax.shard_map(
        on_device, mesh=mesh, in_specs=in_specs, out_specs=out_specs, check_vma=False
    )
```

profile of v0, /device:TPU:0, one launch (start us, length us, event | category | flops | bytes accessed | tf_op | source)
XLA Modules:
  0.0 323.3 jit_solution(16852734257840605443)
XLA Ops:
  7.3 12.0 %copy.8 = bf16[1,1,1024,4096]{2,3,1,0:T(8,128)(2,1)} copy(bf16[1,1,1024,4096]{3,2,1,0:T(8,128)(2,1)} %param.10) | data formatting | bytes 16777216 | tf_op args[1]
  19.4 9.0 %all-gather.2.cloned.1.call-done = bf16[1,2048,256]{2,1,0:T(8,128)(2,1)} async-done(((bf16[1,512,256]{2,1,0:T(8,128)(2,1)}), bf16[1,2048,256]{2,1,0:T(8,128)(2,1)}) %all-gather.2.cloned.1.call-update) | async-done | bytes 1048592 | tf_op jit(solution)/shard_map/all_gather | solution.py:12
  28.4 239.3 %while.14 = (s32[]{:T(128)}, f32[32,16384]{1,0:T(8,128)}, s32[]{:T(128)}, s32[1024]{0:T(1024)}, bf16[1024,64,64]{0,2,1:T(8,128)(2,1)}, /*index=5*/s32[1024]{0:T(...) while((s32[]{:T(128)}, f32[32,16384]{1,0:T(8,128)}, ...), condition=%wide.region_1.2_spmd.clone, body=%wide.region_0.1_spmd.clone.sunk | while | flops 1074796288 | bytes 72359656 | solution.py:46
  28.4 1.4 compare_select_fusion.3
  29.8 4.0 %gather_fusion = bf16[128,64,256]{2,1,0:T(8,128)(2,1)} fusion(bf16[32,64,256]{2,1,0:T(8,128)(2,1)} %get-tuple-element.269, s32[1024]{0:T(1024)S(1)} %pad_clamp_fusion.2), kind=kCustom, calls=%fused_computation.clone.clone.1 | custom fusion | bytes 8389120 | tf_op jit(solution)/shard_map/while/body/eval_jaxpr/gather | solution.py:28
  35.1 3.0 copy.14
  38.1 3.4 %fusion.19 = f32[128,64,256]{2,1,0:T(8,128)S(1)} fusion(bf16[128,64,64]{2,1,0:T(8,128)(2,1)S(1)} %copy.14, bf16[128,64,256]{2,1,0:T(8,128)(2,1)} %gather_fusion), kind=kOutput, calls=%fused_computation.14.clone.1 | convolution fusion | flops 268435456 | bytes 13631488 | tf_op jit(solution)/shard_map/while/body/eval_jaxpr/bij,bjf->bif/dot_general | solution.py:29
  41.5 9.7 %copy.15 = f32[16,8,64,256]{3,1,2,0:T(8,128)} copy(f32[16,8,64,256]{3,2,1,0:T(8,128)S(1)} %bitcast.24) | data formatting | bytes 16777216 | tf_op jit(solution)/shard_map/while
  51.3 5.6 %convolution_add_fusion.3 = f32[32,16384]{1,0:T(8,128)S(1)} fusion(f32[128,16384]{1,0:T(8,128)} %bitcast.23, f32[32,16384]{1,0:T(8,128)S(1)} %copy-done.1, pred[]{:T(512)S(6)} %compare.3, s32[128]{0:T(128)S(1)} %get-tuple-element.240), kind=kOutput, calls=%fused_computation.2.clone.1 | convolution fusion | flops 806359040 | bytes 12583425 | tf_op jit(solution)/shard_map/while/body/eval_jaxpr/dot_general | solution.py:36
  57.0 1.3 copy-done.2
  58.3 1.4 compare_select_fusion.3
  59.7 4.0 %gather_fusion = bf16[128,64,256]{2,1,0:T(8,128)(2,1)} fusion(bf16[32,64,256]{2,1,0:T(8,128)(2,1)} %get-tuple-element.269, s32[1024]{0:T(1024)S(1)} %pad_clamp_fusion.2), kind=kCustom, calls=%fused_computation.clone.clone.1 | custom fusion | bytes 8389120 | tf_op jit(solution)/shard_map/while/body/eval_jaxpr/gather | solution.py:28
  63.7 1.3 constant_dynamic-slice_fusion.2
  65.0 3.0 copy.14
  68.0 3.4 %fusion.19 = f32[128,64,256]{2,1,0:T(8,128)S(1)} fusion(bf16[128,64,64]{2,1,0:T(8,128)(2,1)S(1)} %copy.14, bf16[128,64,256]{2,1,0:T(8,128)(2,1)} %gather_fusion), kind=kOutput, calls=%fused_computation.14.clone.1 | convolution fusion | flops 268435456 | bytes 13631488 | tf_op jit(solution)/shard_map/while/body/eval_jaxpr/bij,bjf->bif/dot_general | solution.py:29
  71.5 9.7 %copy.15 = f32[16,8,64,256]{3,1,2,0:T(8,128)} copy(f32[16,8,64,256]{3,2,1,0:T(8,128)S(1)} %bitcast.24) | data formatting | bytes 16777216 | tf_op jit(solution)/shard_map/while
  81.2 5.6 %convolution_add_fusion.3 = f32[32,16384]{1,0:T(8,128)S(1)} fusion(f32[128,16384]{1,0:T(8,128)} %bitcast.23, f32[32,16384]{1,0:T(8,128)S(1)} %copy-done.1, pred[]{:T(512)S(6)} %compare.3, s32[128]{0:T(128)S(1)} %get-tuple-element.240), kind=kOutput, calls=%fused_computation.2.clone.1 | convolution fusion | flops 806359040 | bytes 12583425 | tf_op jit(solution)/shard_map/while/body/eval_jaxpr/dot_general | solution.py:36
  86.9 1.3 copy-done.2
  88.2 1.4 compare_select_fusion.3
  89.6 4.0 %gather_fusion = bf16[128,64,256]{2,1,0:T(8,128)(2,1)} fusion(bf16[32,64,256]{2,1,0:T(8,128)(2,1)} %get-tuple-element.269, s32[1024]{0:T(1024)S(1)} %pad_clamp_fusion.2), kind=kCustom, calls=%fused_computation.clone.clone.1 | custom fusion | bytes 8389120 | tf_op jit(solution)/shard_map/while/body/eval_jaxpr/gather | solution.py:28
  93.6 1.3 constant_dynamic-slice_fusion.2
  94.9 3.0 copy.14
  97.9 3.4 %fusion.19 = f32[128,64,256]{2,1,0:T(8,128)S(1)} fusion(bf16[128,64,64]{2,1,0:T(8,128)(2,1)S(1)} %copy.14, bf16[128,64,256]{2,1,0:T(8,128)(2,1)} %gather_fusion), kind=kOutput, calls=%fused_computation.14.clone.1 | convolution fusion | flops 268435456 | bytes 13631488 | tf_op jit(solution)/shard_map/while/body/eval_jaxpr/bij,bjf->bif/dot_general | solution.py:29
  101.4 9.7 %copy.15 = f32[16,8,64,256]{3,1,2,0:T(8,128)} copy(f32[16,8,64,256]{3,2,1,0:T(8,128)S(1)} %bitcast.24) | data formatting | bytes 16777216 | tf_op jit(solution)/shard_map/while
  111.1 5.6 %convolution_add_fusion.3 = f32[32,16384]{1,0:T(8,128)S(1)} fusion(f32[128,16384]{1,0:T(8,128)} %bitcast.23, f32[32,16384]{1,0:T(8,128)S(1)} %copy-done.1, pred[]{:T(512)S(6)} %compare.3, s32[128]{0:T(128)S(1)} %get-tuple-element.240), kind=kOutput, calls=%fused_computation.2.clone.1 | convolution fusion | flops 806359040 | bytes 12583425 | tf_op jit(solution)/shard_map/while/body/eval_jaxpr/dot_general | solution.py:36
  116.8 1.3 copy-done.2
  118.1 1.4 compare_select_fusion.3
  119.5 4.0 %gather_fusion = bf16[128,64,256]{2,1,0:T(8,128)(2,1)} fusion(bf16[32,64,256]{2,1,0:T(8,128)(2,1)} %get-tuple-element.269, s32[1024]{0:T(1024)S(1)} %pad_clamp_fusion.2), kind=kCustom, calls=%fused_computation.clone.clone.1 | custom fusion | bytes 8389120 | tf_op jit(solution)/shard_map/while/body/eval_jaxpr/gather | solution.py:28
  124.8 3.0 copy.14
  127.8 3.4 %fusion.19 = f32[128,64,256]{2,1,0:T(8,128)S(1)} fusion(bf16[128,64,64]{2,1,0:T(8,128)(2,1)S(1)} %copy.14, bf16[128,64,256]{2,1,0:T(8,128)(2,1)} %gather_fusion), kind=kOutput, calls=%fused_computation.14.clone.1 | convolution fusion | flops 268435456 | bytes 13631488 | tf_op jit(solution)/shard_map/while/body/eval_jaxpr/bij,bjf->bif/dot_general | solution.py:29
  131.3 9.7 %copy.15 = f32[16,8,64,256]{3,1,2,0:T(8,128)} copy(f32[16,8,64,256]{3,2,1,0:T(8,128)S(1)} %bitcast.24) | data formatting | bytes 16777216 | tf_op jit(solution)/shard_map/while
  141.0 5.6 %convolution_add_fusion.3 = f32[32,16384]{1,0:T(8,128)S(1)} fusion(f32[128,16384]{1,0:T(8,128)} %bitcast.23, f32[32,16384]{1,0:T(8,128)S(1)} %copy-done.1, pred[]{:T(512)S(6)} %compare.3, s32[128]{0:T(128)S(1)} %get-tuple-element.240), kind=kOutput, calls=%fused_computation.2.clone.1 | convolution fusion | flops 806359040 | bytes 12583425 | tf_op jit(solution)/shard_map/while/body/eval_jaxpr/dot_general | solution.py:36
  146.7 1.3 copy-done.2
  148.0 1.4 compare_select_fusion.3
  149.4 4.0 %gather_fusion = bf16[128,64,256]{2,1,0:T(8,128)(2,1)} fusion(bf16[32,64,256]{2,1,0:T(8,128)(2,1)} %get-tuple-element.269, s32[1024]{0:T(1024)S(1)} %pad_clamp_fusion.2), kind=kCustom, calls=%fused_computation.clone.clone.1 | custom fusion | bytes 8389120 | tf_op jit(solution)/shard_map/while/body/eval_jaxpr/gather | solution.py:28
  154.7 3.0 copy.14
  157.7 3.4 %fusion.19 = f32[128,64,256]{2,1,0:T(8,128)S(1)} fusion(bf16[128,64,64]{2,1,0:T(8,128)(2,1)S(1)} %copy.14, bf16[128,64,256]{2,1,0:T(8,128)(2,1)} %gather_fusion), kind=kOutput, calls=%fused_computation.14.clone.1 | convolution fusion | flops 268435456 | bytes 13631488 | tf_op jit(solution)/shard_map/while/body/eval_jaxpr/bij,bjf->bif/dot_general | solution.py:29
  161.2 9.7 %copy.15 = f32[16,8,64,256]{3,1,2,0:T(8,128)} copy(f32[16,8,64,256]{3,2,1,0:T(8,128)S(1)} %bitcast.24) | data formatting | bytes 16777216 | tf_op jit(solution)/shard_map/while
  170.9 5.6 %convolution_add_fusion.3 = f32[32,16384]{1,0:T(8,128)S(1)} fusion(f32[128,16384]{1,0:T(8,128)} %bitcast.23, f32[32,16384]{1,0:T(8,128)S(1)} %copy-done.1, pred[]{:T(512)S(6)} %compare.3, s32[128]{0:T(128)S(1)} %get-tuple-element.240), kind=kOutput, calls=%fused_computation.2.clone.1 | convolution fusion | flops 806359040 | bytes 12583425 | tf_op jit(solution)/shard_map/while/body/eval_jaxpr/dot_general | solution.py:36
  176.6 1.3 copy-done.2
  177.9 1.4 compare_select_fusion.3
  179.3 4.0 %gather_fusion = bf16[128,64,256]{2,1,0:T(8,128)(2,1)} fusion(bf16[32,64,256]{2,1,0:T(8,128)(2,1)} %get-tuple-element.269, s32[1024]{0:T(1024)S(1)} %pad_clamp_fusion.2), kind=kCustom, calls=%fused_computation.clone.clone.1 | custom fusion | bytes 8389120 | tf_op jit(solution)/shard_map/while/body/eval_jaxpr/gather | solution.py:28
  184.7 3.0 copy.14
  187.7 3.4 %fusion.19 = f32[128,64,256]{2,1,0:T(8,128)S(1)} fusion(bf16[128,64,64]{2,1,0:T(8,128)(2,1)S(1)} %copy.14, bf16[128,64,256]{2,1,0:T(8,128)(2,1)} %gather_fusion), kind=kOutput, calls=%fused_computation.14.clone.1 | convolution fusion | flops 268435456 | bytes 13631488 | tf_op jit(solution)/shard_map/while/body/eval_jaxpr/bij,bjf->bif/dot_general | solution.py:29
  191.1 9.7 %copy.15 = f32[16,8,64,256]{3,1,2,0:T(8,128)} copy(f32[16,8,64,256]{3,2,1,0:T(8,128)S(1)} %bitcast.24) | data formatting | bytes 16777216 | tf_op jit(solution)/shard_map/while
  200.8 5.6 %convolution_add_fusion.3 = f32[32,16384]{1,0:T(8,128)S(1)} fusion(f32[128,16384]{1,0:T(8,128)} %bitcast.23, f32[32,16384]{1,0:T(8,128)S(1)} %copy-done.1, pred[]{:T(512)S(6)} %compare.3, s32[128]{0:T(128)S(1)} %get-tuple-element.240), kind=kOutput, calls=%fused_computation.2.clone.1 | convolution fusion | flops 806359040 | bytes 12583425 | tf_op jit(solution)/shard_map/while/body/eval_jaxpr/dot_general | solution.py:36
  206.5 1.3 copy-done.2
  207.8 1.4 compare_select_fusion.3
  209.3 4.0 %gather_fusion = bf16[128,64,256]{2,1,0:T(8,128)(2,1)} fusion(bf16[32,64,256]{2,1,0:T(8,128)(2,1)} %get-tuple-element.269, s32[1024]{0:T(1024)S(1)} %pad_clamp_fusion.2), kind=kCustom, calls=%fused_computation.clone.clone.1 | custom fusion | bytes 8389120 | tf_op jit(solution)/shard_map/while/body/eval_jaxpr/gather | solution.py:28
  214.6 3.0 copy.14
  217.6 3.4 %fusion.19 = f32[128,64,256]{2,1,0:T(8,128)S(1)} fusion(bf16[128,64,64]{2,1,0:T(8,128)(2,1)S(1)} %copy.14, bf16[128,64,256]{2,1,0:T(8,128)(2,1)} %gather_fusion), kind=kOutput, calls=%fused_computation.14.clone.1 | convolution fusion | flops 268435456 | bytes 13631488 | tf_op jit(solution)/shard_map/while/body/eval_jaxpr/bij,bjf->bif/dot_general | solution.py:29
  221.0 9.7 %copy.15 = f32[16,8,64,256]{3,1,2,0:T(8,128)} copy(f32[16,8,64,256]{3,2,1,0:T(8,128)S(1)} %bitcast.24) | data formatting | bytes 16777216 | tf_op jit(solution)/shard_map/while
  230.7 5.6 %convolution_add_fusion.3 = f32[32,16384]{1,0:T(8,128)S(1)} fusion(f32[128,16384]{1,0:T(8,128)} %bitcast.23, f32[32,16384]{1,0:T(8,128)S(1)} %copy-done.1, pred[]{:T(512)S(6)} %compare.3, s32[128]{0:T(128)S(1)} %get-tuple-element.240), kind=kOutput, calls=%fused_computation.2.clone.1 | convolution fusion | flops 806359040 | bytes 12583425 | tf_op jit(solution)/shard_map/while/body/eval_jaxpr/dot_general | solution.py:36
  236.4 1.3 copy-done.2
  237.7 1.4 compare_select_fusion.3
  239.2 4.0 %gather_fusion = bf16[128,64,256]{2,1,0:T(8,128)(2,1)} fusion(bf16[32,64,256]{2,1,0:T(8,128)(2,1)} %get-tuple-element.269, s32[1024]{0:T(1024)S(1)} %pad_clamp_fusion.2), kind=kCustom, calls=%fused_computation.clone.clone.1 | custom fusion | bytes 8389120 | tf_op jit(solution)/shard_map/while/body/eval_jaxpr/gather | solution.py:28
  244.5 3.0 copy.14
  247.5 3.4 %fusion.19 = f32[128,64,256]{2,1,0:T(8,128)S(1)} fusion(bf16[128,64,64]{2,1,0:T(8,128)(2,1)S(1)} %copy.14, bf16[128,64,256]{2,1,0:T(8,128)(2,1)} %gather_fusion), kind=kOutput, calls=%fused_computation.14.clone.1 | convolution fusion | flops 268435456 | bytes 13631488 | tf_op jit(solution)/shard_map/while/body/eval_jaxpr/bij,bjf->bif/dot_general | solution.py:29
  250.9 9.7 %copy.15 = f32[16,8,64,256]{3,1,2,0:T(8,128)} copy(f32[16,8,64,256]{3,2,1,0:T(8,128)S(1)} %bitcast.24) | data formatting | bytes 16777216 | tf_op jit(solution)/shard_map/while
  260.6 5.6 %convolution_add_fusion.3 = f32[32,16384]{1,0:T(8,128)S(1)} fusion(f32[128,16384]{1,0:T(8,128)} %bitcast.23, f32[32,16384]{1,0:T(8,128)S(1)} %copy-done.1, pred[]{:T(512)S(6)} %compare.3, s32[128]{0:T(128)S(1)} %get-tuple-element.240), kind=kOutput, calls=%fused_computation.2.clone.1 | convolution fusion | flops 806359040 | bytes 12583425 | tf_op jit(solution)/shard_map/while/body/eval_jaxpr/dot_general | solution.py:36
  266.3 1.3 copy-done.2
  267.6 2.7 reshape.36
  270.4 44.0 %reduce-scatter.2.cloned.1.call-done = f32[512,256]{1,0:T(8,128)} async-done(((f32[2048,256]{1,0:T(8,128)}), f32[512,256]{1,0:T(8,128)}) %reduce-scatter.2.cloned.1.call-update) | async-done | bytes 524304 | tf_op jit(solution)/shard_map/reduce_scatter | solution.py:48
  314.4 2.0 fusion.5
  (47 shorter events, 8.6 us)
Async XLA Ops:
  6.5 307.9 %copy-start = (bf16[256,256]{1,0:T(8,128)(2,1)S(1)}, bf16[256,256]{1,0:T(8,128)(2,1)}, u32[]{:S(2)}) copy-start(bf16[256,256]{1,0:T(8,128)(2,1)} %param.14) | copy-start | bytes 393220
  6.5 21.8 %all-gather.2.cloned.1.call-start = ((), (), s32[]{:S(2)}) async-start(), calls=%async_computation.1 | async-start | bytes 1310720 | tf_op jit(solution)/shard_map/all_gather | solution.py:12
  7.3 307.2 %reduce-scatter.2.cloned.1.call-start = ((), (), s32[]{:S(2)}) async-start(), calls=%async_computation.2 | async-start | bytes 2621440 | tf_op jit(solution)/shard_map/reduce_scatter | solution.py:48
  41.5 9.7 %copy-start.1 = (f32[32,16384]{1,0:T(8,128)S(1)}, f32[32,16384]{1,0:T(8,128)}, u32[]{:S(2)}) copy-start(f32[32,16384]{1,0:T(8,128)} %get-tuple-element.253) | copy-start | bytes 6291460 | tf_op jit(solution)/shard_map/while
  56.9 1.3 copy-start.2
  71.4 9.7 %copy-start.1 = (f32[32,16384]{1,0:T(8,128)S(1)}, f32[32,16384]{1,0:T(8,128)}, u32[]{:S(2)}) copy-start(f32[32,16384]{1,0:T(8,128)} %get-tuple-element.253) | copy-start | bytes 6291460 | tf_op jit(solution)/shard_map/while
  86.8 1.3 copy-start.2
  101.4 9.7 %copy-start.1 = (f32[32,16384]{1,0:T(8,128)S(1)}, f32[32,16384]{1,0:T(8,128)}, u32[]{:S(2)}) copy-start(f32[32,16384]{1,0:T(8,128)} %get-tuple-element.253) | copy-start | bytes 6291460 | tf_op jit(solution)/shard_map/while
  116.8 1.3 copy-start.2
  131.3 9.7 %copy-start.1 = (f32[32,16384]{1,0:T(8,128)S(1)}, f32[32,16384]{1,0:T(8,128)}, u32[]{:S(2)}) copy-start(f32[32,16384]{1,0:T(8,128)} %get-tuple-element.253) | copy-start | bytes 6291460 | tf_op jit(solution)/shard_map/while
  146.7 1.3 copy-start.2
  161.2 9.7 %copy-start.1 = (f32[32,16384]{1,0:T(8,128)S(1)}, f32[32,16384]{1,0:T(8,128)}, u32[]{:S(2)}) copy-start(f32[32,16384]{1,0:T(8,128)} %get-tuple-element.253) | copy-start | bytes 6291460 | tf_op jit(solution)/shard_map/while
  176.6 1.3 copy-start.2
  191.1 9.7 %copy-start.1 = (f32[32,16384]{1,0:T(8,128)S(1)}, f32[32,16384]{1,0:T(8,128)}, u32[]{:S(2)}) copy-start(f32[32,16384]{1,0:T(8,128)} %get-tuple-element.253) | copy-start | bytes 6291460 | tf_op jit(solution)/shard_map/while
  206.5 1.3 copy-start.2
  221.0 9.7 %copy-start.1 = (f32[32,16384]{1,0:T(8,128)S(1)}, f32[32,16384]{1,0:T(8,128)}, u32[]{:S(2)}) copy-start(f32[32,16384]{1,0:T(8,128)} %get-tuple-element.253) | copy-start | bytes 6291460 | tf_op jit(solution)/shard_map/while
  236.4 1.3 copy-start.2
  250.9 9.7 %copy-start.1 = (f32[32,16384]{1,0:T(8,128)S(1)}, f32[32,16384]{1,0:T(8,128)}, u32[]{:S(2)}) copy-start(f32[32,16384]{1,0:T(8,128)} %get-tuple-element.253) | copy-start | bytes 6291460 | tf_op jit(solution)/shard_map/while
  266.3 1.3 copy-start.2
  267.6 46.8 %copy-start.3 = (f32[256]{0:T(256)S(1)}, f32[256]{0:T(256)}, u32[]{:S(2)}) copy-start(f32[256]{0:T(256)} %param.15) | copy-start | bytes 3076
Sparse Core Ops, SparseCore 0:
  8.9 19.4 all-gather.1
  270.5 43.8 reduce-scatter.1
where the time goes:
time: 325 us; the launch traced here: 323 us
  local copies, waits for them, and re-layouts  170 us (52%)
  matrix products  74.5 us (23%)
  waiting for transfers between devices  53.8 us (17%)
  between operations  13.4 us (4%)
  other arithmetic  11.4 us (4%)
    while x40, local copies, waits for them, and re-layouts  88.5 us
    dot_general x8, matrix products, block_step(): jnp.dot(selector, flat_products, precision=lax.Precision.HIGHEST, preferr...  45.2 us
    reduce_scatter x1, waiting for transfers between devices, on_device(): lax.psum_scatter(partial_value, 'row', scatter_dimension=0, tiled=True)  44 us
    dynamic_slice x16, local copies, waits for them, and re-layouts, block_step(): tile_block = lax.dynamic_slice_in_dim(values, first_slot, block_size, 0)  34.2 us
    gather x8, local copies, waits for them, and re-layouts, block_step(): inputs = source[source_cols]  32.1 us
    dot_general x8, matrix products, block_step(): jnp.einsum('bij,bjf->bif', tile_block, inputs, preferred_element_type=jnp...  27.4 us
    unnamed x5, local copies, waits for them, and re-layouts  12 us
    select_n x8, other arithmetic, block_step(): inputs = source[source_cols]  11.4 us
  transfers between devices with their start and end apart: 2, of which 2 were waited for; matrix products, arithmetic and copies ran while one was open for 4% of the time, Pallas kernels for 0%

commit v1 on v0

--- a/solution.py
+++ b/solution.py
@@ -9,7 +9,14 @@
 def on_device(features, tile_values, tile_rows, tile_cols, counts, weight, bias):
     piece_rows = features.shape[1]
     feat_width = features.shape[2]
-    gathered = lax.all_gather(features, "col", axis=1, tiled=True)
+    ways, here, step = (lax.axis_size("col"), lax.axis_index("col"), features.shape[1])
+    line, have = (features, 1)
+    while have < ways:
+        line = jnp.concatenate(
+            [line, lax.ppermute(line, "col", [(d, (d - have) % ways) for d in range(ways)])], axis=1
+        )
+        have = 2 * have
+    gathered = jnp.roll(line, here * step, axis=1)
     source = gathered.reshape(-1, TILE, feat_width)
     slot_count = tile_values.shape[2]
     block_size = min(128, slot_count)

time: 325 us -> 332 us (1.022)
  local copies, waits for them, and re-layouts: 170 us -> 176 us
  waiting for transfers between devices: 53.8 us -> 50.4 us
    dynamic_slice x16, local copies, waits for them, and re-layouts: 34.2 us -> 50.1 us  [block_step(): tile_block = lax.dynamic_slice_in_dim(values, first_slot, block_size, 0)]
    gather x8, local copies, waits for them, and re-layouts: 32.1 us -> 22.3 us  [block_step(): inputs = source[source_cols]]
    all_gather x1 -> x0, waiting for transfers between devices: 9.02 us -> none  [on_device(): gathered = lax.all_gather(features, 'col', axis=1, tiled=True)]
    ppermute x0 -> x2, waiting for transfers between devices: none -> 6.11 us  [on_device(): lax.ppermute(line, 'col', [(d, (d - have) % ways) for d in range(ways)])]
    unnamed x5 -> x12, local copies, waits for them, and re-layouts: 12 us -> 12.2 us
  transfers between devices with their start and end apart: 2 -> 3, of which waited for: 2 -> 3; matrix products, arithmetic and copies ran while one was open for 4% -> 4% of each run, Pallas kernels for 0% -> 0%
where the time goes in v1:
time: 332 us; the launch traced here: 330 us
  local copies, waits for them, and re-layouts  176 us (53%)
  matrix products  74.5 us (22%)
  waiting for transfers between devices  50.4 us (15%)
  between operations  13.4 us (4%)
  other arithmetic  12.4 us (4%)
    while x40, local copies, waits for them, and re-layouts  88.5 us
    dynamic_slice x16, local copies, waits for them, and re-layouts, block_step(): tile_block = lax.dynamic_slice_in_dim(values, first_slot, block_size, 0)  50.1 us
    dot_general x8, matrix products, block_step(): jnp.dot(selector, flat_products, precision=lax.Precision.HIGHEST, preferr...  45.2 us
    reduce_scatter x1, waiting for transfers between devices, on_device(): lax.psum_scatter(partial_value, 'row', scatter_dimension=0, tiled=True)  44.3 us
    dot_general x8, matrix products, block_step(): jnp.einsum('bij,bjf->bif', tile_block, inputs, preferred_element_type=jnp...  27.4 us
    gather x8, local copies, waits for them, and re-layouts, block_step(): inputs = source[source_cols]  22.3 us
    unnamed x12, local copies, waits for them, and re-layouts  12.2 us
    select_n x8, other arithmetic, block_step(): inputs = source[source_cols]  11.4 us
  transfers between devices with their start and end apart: 3, of which 3 were waited for; matrix products, arithmetic and copies ran while one was open for 4% of the time, Pallas kernels for 0%

profile of v1, /device:TPU:0, one launch (start us, length us, event | category | flops | bytes accessed | tf_op | source)
XLA Modules:
  0.0 330.2 jit_solution(37916591541317909)
XLA Ops:
  6.5 2.4 collective-permute-start
  8.9 4.2 %collective-permute-done = bf16[1,512,256]{2,1,0:T(8,128)(2,1)S(1)} collective-permute-done((bf16[1,512,256]{2,1,0:T(8,128)(2,1)}, bf16[1,512,256]{2,1,0:T(8,128)(2,1)S(1)}, u32[]{:S(2)}, u32[]{:S(2)}) %collective-permute-start) | collective-permute-done | bytes 262176 | tf_op jit(solution)/shard_map/ppermute | solution.py:16
  14.7 12.0 %copy.8 = bf16[1,1,1024,4096]{2,3,1,0:T(8,128)(2,1)} copy(bf16[1,1,1024,4096]{3,2,1,0:T(8,128)(2,1)} %param.10) | data formatting | bytes 16777216 | tf_op args[1]
  26.8 1.9 collective-permute-done.1
  29.0 245.3 %while.14 = (s32[]{:T(128)}, f32[32,16384]{1,0:T(8,128)}, s32[]{:T(128)}, s32[1024]{0:T(1024)}, bf16[1024,64,64]{0,2,1:T(8,128)(2,1)}, /*index=5*/s32[1024]{0:T(...) while((s32[]{:T(128)}, f32[32,16384]{1,0:T(8,128)}, ...), condition=%wide.region_1.2_spmd.clone, body=%wide.region_0.1_spmd.clone.sunk | while | flops 1074796288 | bytes 72359656 | solution.py:53
  29.0 1.4 compare_select_fusion.3
  30.4 2.8 gather_fusion
  33.2 2.3 constant_dynamic-slice_fusion.3
  35.5 3.9 %copy.14 = bf16[128,64,64]{2,1,0:T(8,128)(2,1)S(1)} copy(bf16[128,64,64]{0,2,1:T(8,128)(2,1)} %constant_dynamic-slice_fusion.3) | data formatting | bytes 2097152 | tf_op jit(solution)/shard_map/while/body/eval_jaxpr/dynamic_slice | solution.py:32
  39.5 3.4 %fusion.19 = f32[128,64,256]{2,1,0:T(8,128)S(1)} fusion(bf16[128,64,64]{2,1,0:T(8,128)(2,1)S(1)} %copy.14, bf16[128,64,256]{2,1,0:T(8,128)(2,1)} %gather_fusion), kind=kOutput, calls=%fused_computation.22.clone.1 | convolution fusion | flops 268435456 | bytes 13631488 | tf_op jit(solution)/shard_map/while/body/eval_jaxpr/bij,bjf->bif/dot_general | solution.py:36
  42.9 9.7 %copy.15 = f32[16,8,64,256]{3,1,2,0:T(8,128)} copy(f32[16,8,64,256]{3,2,1,0:T(8,128)S(1)} %bitcast.24) | data formatting | bytes 16777216 | tf_op jit(solution)/shard_map/while
  52.7 5.6 %convolution_add_fusion.3 = f32[32,16384]{1,0:T(8,128)S(1)} fusion(f32[128,16384]{1,0:T(8,128)} %bitcast.23, f32[32,16384]{1,0:T(8,128)S(1)} %copy-done.1, pred[]{:T(512)S(6)} %compare.4, s32[128]{0:T(128)S(1)} %get-tuple-element.240), kind=kOutput, calls=%fused_computation.2.clone.1 | convolution fusion | flops 806359040 | bytes 12583425 | tf_op jit(solution)/shard_map/while/body/eval_jaxpr/dot_general | solution.py:43
  59.6 1.4 compare_select_fusion.3
  61.1 2.8 gather_fusion
  63.9 2.3 constant_dynamic-slice_fusion.3
  66.2 3.9 %copy.14 = bf16[128,64,64]{2,1,0:T(8,128)(2,1)S(1)} copy(bf16[128,64,64]{0,2,1:T(8,128)(2,1)} %constant_dynamic-slice_fusion.3) | data formatting | bytes 2097152 | tf_op jit(solution)/shard_map/while/body/eval_jaxpr/dynamic_slice | solution.py:32
  70.1 3.4 %fusion.19 = f32[128,64,256]{2,1,0:T(8,128)S(1)} fusion(bf16[128,64,64]{2,1,0:T(8,128)(2,1)S(1)} %copy.14, bf16[128,64,256]{2,1,0:T(8,128)(2,1)} %gather_fusion), kind=kOutput, calls=%fused_computation.22.clone.1 | convolution fusion | flops 268435456 | bytes 13631488 | tf_op jit(solution)/shard_map/while/body/eval_jaxpr/bij,bjf->bif/dot_general | solution.py:36
  73.6 9.7 %copy.15 = f32[16,8,64,256]{3,1,2,0:T(8,128)} copy(f32[16,8,64,256]{3,2,1,0:T(8,128)S(1)} %bitcast.24) | data formatting | bytes 16777216 | tf_op jit(solution)/shard_map/while
  83.3 5.6 %convolution_add_fusion.3 = f32[32,16384]{1,0:T(8,128)S(1)} fusion(f32[128,16384]{1,0:T(8,128)} %bitcast.23, f32[32,16384]{1,0:T(8,128)S(1)} %copy-done.1, pred[]{:T(512)S(6)} %compare.4, s32[128]{0:T(128)S(1)} %get-tuple-element.240), kind=kOutput, calls=%fused_computation.2.clone.1 | convolution fusion | flops 806359040 | bytes 12583425 | tf_op jit(solution)/shard_map/while/body/eval_jaxpr/dot_general | solution.py:43
  90.3 1.4 compare_select_fusion.3
  91.8 2.8 gather_fusion
  94.5 2.3 constant_dynamic-slice_fusion.3
  96.9 3.9 %copy.14 = bf16[128,64,64]{2,1,0:T(8,128)(2,1)S(1)} copy(bf16[128,64,64]{0,2,1:T(8,128)(2,1)} %constant_dynamic-slice_fusion.3) | data formatting | bytes 2097152 | tf_op jit(solution)/shard_map/while/body/eval_jaxpr/dynamic_slice | solution.py:32
  100.8 3.4 %fusion.19 = f32[128,64,256]{2,1,0:T(8,128)S(1)} fusion(bf16[128,64,64]{2,1,0:T(8,128)(2,1)S(1)} %copy.14, bf16[128,64,256]{2,1,0:T(8,128)(2,1)} %gather_fusion), kind=kOutput, calls=%fused_computation.22.clone.1 | convolution fusion | flops 268435456 | bytes 13631488 | tf_op jit(solution)/shard_map/while/body/eval_jaxpr/bij,bjf->bif/dot_general | solution.py:36
  104.2 9.7 %copy.15 = f32[16,8,64,256]{3,1,2,0:T(8,128)} copy(f32[16,8,64,256]{3,2,1,0:T(8,128)S(1)} %bitcast.24) | data formatting | bytes 16777216 | tf_op jit(solution)/shard_map/while
  114.0 5.6 %convolution_add_fusion.3 = f32[32,16384]{1,0:T(8,128)S(1)} fusion(f32[128,16384]{1,0:T(8,128)} %bitcast.23, f32[32,16384]{1,0:T(8,128)S(1)} %copy-done.1, pred[]{:T(512)S(6)} %compare.4, s32[128]{0:T(128)S(1)} %get-tuple-element.240), kind=kOutput, calls=%fused_computation.2.clone.1 | convolution fusion | flops 806359040 | bytes 12583425 | tf_op jit(solution)/shard_map/while/body/eval_jaxpr/dot_general | solution.py:43
  121.0 1.4 compare_select_fusion.3
  122.4 2.8 gather_fusion
  125.2 2.3 constant_dynamic-slice_fusion.3
  127.5 3.9 %copy.14 = bf16[128,64,64]{2,1,0:T(8,128)(2,1)S(1)} copy(bf16[128,64,64]{0,2,1:T(8,128)(2,1)} %constant_dynamic-slice_fusion.3) | data formatting | bytes 2097152 | tf_op jit(solution)/shard_map/while/body/eval_jaxpr/dynamic_slice | solution.py:32
  131.5 3.4 %fusion.19 = f32[128,64,256]{2,1,0:T(8,128)S(1)} fusion(bf16[128,64,64]{2,1,0:T(8,128)(2,1)S(1)} %copy.14, bf16[128,64,256]{2,1,0:T(8,128)(2,1)} %gather_fusion), kind=kOutput, calls=%fused_computation.22.clone.1 | convolution fusion | flops 268435456 | bytes 13631488 | tf_op jit(solution)/shard_map/while/body/eval_jaxpr/bij,bjf->bif/dot_general | solution.py:36
  134.9 9.7 %copy.15 = f32[16,8,64,256]{3,1,2,0:T(8,128)} copy(f32[16,8,64,256]{3,2,1,0:T(8,128)S(1)} %bitcast.24) | data formatting | bytes 16777216 | tf_op jit(solution)/shard_map/while
  144.7 5.6 %convolution_add_fusion.3 = f32[32,16384]{1,0:T(8,128)S(1)} fusion(f32[128,16384]{1,0:T(8,128)} %bitcast.23, f32[32,16384]{1,0:T(8,128)S(1)} %copy-done.1, pred[]{:T(512)S(6)} %compare.4, s32[128]{0:T(128)S(1)} %get-tuple-element.240), kind=kOutput, calls=%fused_computation.2.clone.1 | convolution fusion | flops 806359040 | bytes 12583425 | tf_op jit(solution)/shard_map/while/body/eval_jaxpr/dot_general | solution.py:43
  151.6 1.4 compare_select_fusion.3
  153.1 2.8 gather_fusion
  155.9 2.3 constant_dynamic-slice_fusion.3
  158.2 3.9 %copy.14 = bf16[128,64,64]{2,1,0:T(8,128)(2,1)S(1)} copy(bf16[128,64,64]{0,2,1:T(8,128)(2,1)} %constant_dynamic-slice_fusion.3) | data formatting | bytes 2097152 | tf_op jit(solution)/shard_map/while/body/eval_jaxpr/dynamic_slice | solution.py:32
  162.1 3.4 %fusion.19 = f32[128,64,256]{2,1,0:T(8,128)S(1)} fusion(bf16[128,64,64]{2,1,0:T(8,128)(2,1)S(1)} %copy.14, bf16[128,64,256]{2,1,0:T(8,128)(2,1)} %gather_fusion), kind=kOutput, calls=%fused_computation.22.clone.1 | convolution fusion | flops 268435456 | bytes 13631488 | tf_op jit(solution)/shard_map/while/body/eval_jaxpr/bij,bjf->bif/dot_general | solution.py:36
  165.6 9.7 %copy.15 = f32[16,8,64,256]{3,1,2,0:T(8,128)} copy(f32[16,8,64,256]{3,2,1,0:T(8,128)S(1)} %bitcast.24) | data formatting | bytes 16777216 | tf_op jit(solution)/shard_map/while
  175.3 5.6 %convolution_add_fusion.3 = f32[32,16384]{1,0:T(8,128)S(1)} fusion(f32[128,16384]{1,0:T(8,128)} %bitcast.23, f32[32,16384]{1,0:T(8,128)S(1)} %copy-done.1, pred[]{:T(512)S(6)} %compare.4, s32[128]{0:T(128)S(1)} %get-tuple-element.240), kind=kOutput, calls=%fused_computation.2.clone.1 | convolution fusion | flops 806359040 | bytes 12583425 | tf_op jit(solution)/shard_map/while/body/eval_jaxpr/dot_general | solution.py:43
  182.3 1.4 compare_select_fusion.3
  183.7 2.8 gather_fusion
  186.5 2.3 constant_dynamic-slice_fusion.3
  188.9 3.9 %copy.14 = bf16[128,64,64]{2,1,0:T(8,128)(2,1)S(1)} copy(bf16[128,64,64]{0,2,1:T(8,128)(2,1)} %constant_dynamic-slice_fusion.3) | data formatting | bytes 2097152 | tf_op jit(solution)/shard_map/while/body/eval_jaxpr/dynamic_slice | solution.py:32
  192.8 3.4 %fusion.19 = f32[128,64,256]{2,1,0:T(8,128)S(1)} fusion(bf16[128,64,64]{2,1,0:T(8,128)(2,1)S(1)} %copy.14, bf16[128,64,256]{2,1,0:T(8,128)(2,1)} %gather_fusion), kind=kOutput, calls=%fused_computation.22.clone.1 | convolution fusion | flops 268435456 | bytes 13631488 | tf_op jit(solution)/shard_map/while/body/eval_jaxpr/bij,bjf->bif/dot_general | solution.py:36
  196.2 9.7 %copy.15 = f32[16,8,64,256]{3,1,2,0:T(8,128)} copy(f32[16,8,64,256]{3,2,1,0:T(8,128)S(1)} %bitcast.24) | data formatting | bytes 16777216 | tf_op jit(solution)/shard_map/while
  206.0 5.6 %convolution_add_fusion.3 = f32[32,16384]{1,0:T(8,128)S(1)} fusion(f32[128,16384]{1,0:T(8,128)} %bitcast.23, f32[32,16384]{1,0:T(8,128)S(1)} %copy-done.1, pred[]{:T(512)S(6)} %compare.4, s32[128]{0:T(128)S(1)} %get-tuple-element.240), kind=kOutput, calls=%fused_computation.2.clone.1 | convolution fusion | flops 806359040 | bytes 12583425 | tf_op jit(solution)/shard_map/while/body/eval_jaxpr/dot_general | solution.py:43
  213.0 1.4 compare_select_fusion.3
  214.4 2.8 gather_fusion
  217.2 2.3 constant_dynamic-slice_fusion.3
  219.5 3.9 %copy.14 = bf16[128,64,64]{2,1,0:T(8,128)(2,1)S(1)} copy(bf16[128,64,64]{0,2,1:T(8,128)(2,1)} %constant_dynamic-slice_fusion.3) | data formatting | bytes 2097152 | tf_op jit(solution)/shard_map/while/body/eval_jaxpr/dynamic_slice | solution.py:32
  223.5 3.4 %fusion.19 = f32[128,64,256]{2,1,0:T(8,128)S(1)} fusion(bf16[128,64,64]{2,1,0:T(8,128)(2,1)S(1)} %copy.14, bf16[128,64,256]{2,1,0:T(8,128)(2,1)} %gather_fusion), kind=kOutput, calls=%fused_computation.22.clone.1 | convolution fusion | flops 268435456 | bytes 13631488 | tf_op jit(solution)/shard_map/while/body/eval_jaxpr/bij,bjf->bif/dot_general | solution.py:36
  226.9 9.7 %copy.15 = f32[16,8,64,256]{3,1,2,0:T(8,128)} copy(f32[16,8,64,256]{3,2,1,0:T(8,128)S(1)} %bitcast.24) | data formatting | bytes 16777216 | tf_op jit(solution)/shard_map/while
  236.7 5.6 %convolution_add_fusion.3 = f32[32,16384]{1,0:T(8,128)S(1)} fusion(f32[128,16384]{1,0:T(8,128)} %bitcast.23, f32[32,16384]{1,0:T(8,128)S(1)} %copy-done.1, pred[]{:T(512)S(6)} %compare.4, s32[128]{0:T(128)S(1)} %get-tuple-element.240), kind=kOutput, calls=%fused_computation.2.clone.1 | convolution fusion | flops 806359040 | bytes 12583425 | tf_op jit(solution)/shard_map/while/body/eval_jaxpr/dot_general | solution.py:43
  243.6 1.4 compare_select_fusion.3
  245.1 2.8 gather_fusion
  247.9 2.3 constant_dynamic-slice_fusion.3
  250.2 3.9 %copy.14 = bf16[128,64,64]{2,1,0:T(8,128)(2,1)S(1)} copy(bf16[128,64,64]{0,2,1:T(8,128)(2,1)} %constant_dynamic-slice_fusion.3) | data formatting | bytes 2097152 | tf_op jit(solution)/shard_map/while/body/eval_jaxpr/dynamic_slice | solution.py:32
  254.1 3.4 %fusion.19 = f32[128,64,256]{2,1,0:T(8,128)S(1)} fusion(bf16[128,64,64]{2,1,0:T(8,128)(2,1)S(1)} %copy.14, bf16[128,64,256]{2,1,0:T(8,128)(2,1)} %gather_fusion), kind=kOutput, calls=%fused_computation.22.clone.1 | convolution fusion | flops 268435456 | bytes 13631488 | tf_op jit(solution)/shard_map/while/body/eval_jaxpr/bij,bjf->bif/dot_general | solution.py:36
  257.6 9.7 %copy.15 = f32[16,8,64,256]{3,1,2,0:T(8,128)} copy(f32[16,8,64,256]{3,2,1,0:T(8,128)S(1)} %bitcast.24) | data formatting | bytes 16777216 | tf_op jit(solution)/shard_map/while
  267.3 5.6 %convolution_add_fusion.3 = f32[32,16384]{1,0:T(8,128)S(1)} fusion(f32[128,16384]{1,0:T(8,128)} %bitcast.23, f32[32,16384]{1,0:T(8,128)S(1)} %copy-done.1, pred[]{:T(512)S(6)} %compare.4, s32[128]{0:T(128)S(1)} %get-tuple-element.240), kind=kOutput, calls=%fused_computation.2.clone.1 | convolution fusion | flops 806359040 | bytes 12583425 | tf_op jit(solution)/shard_map/while/body/eval_jaxpr/dot_general | solution.py:43
  274.3 2.7 reshape.36
  277.1 44.3 %reduce-scatter.2.cloned.1.call-done = f32[512,256]{1,0:T(8,128)} async-done(((f32[2048,256]{1,0:T(8,128)}), f32[512,256]{1,0:T(8,128)}) %reduce-scatter.2.cloned.1.call-update) | async-done | bytes 524304 | tf_op jit(solution)/shard_map/reduce_scatter | solution.py:55
  321.4 2.0 fusion.5
  (58 shorter events, 12.6 us)
Async XLA Ops:
  6.5 314.8 %copy-start = (bf16[256,256]{1,0:T(8,128)(2,1)S(1)}, bf16[256,256]{1,0:T(8,128)(2,1)}, u32[]{:S(2)}) copy-start(bf16[256,256]{1,0:T(8,128)(2,1)} %param.14) | copy-start | bytes 393220
  6.5 314.8 %reduce-scatter.2.cloned.1.call-start = ((), (), s32[]{:S(2)}) async-start(), calls=%async_computation.1 | async-start | bytes 2621440 | tf_op jit(solution)/shard_map/reduce_scatter | solution.py:55
  6.5 6.6 %collective-permute-start = (bf16[1,512,256]{2,1,0:T(8,128)(2,1)}, bf16[1,512,256]{2,1,0:T(8,128)(2,1)S(1)}, u32[]{:S(2)}, u32[]{:S(2)}) collective-permute-start(bf16[1,512,256]{2,1,0:T(8,128)(2,1)} %param.9), channel_id=1, source_target_pairs={{0,3},{1,0},{2,1},{3,2},{4,7},{5,4},{6,5},{7,6},{8,11},{9,8},{10,9... | collective-permute-start | bytes 786440 | tf_op jit(solution)/shard_map/ppermute | solution.py:16
  14.1 14.6 %collective-permute-start.1 = (bf16[1,1024,256]{2,1,0:T(8,128)(2,1)S(1)}, bf16[1,1024,256]{2,1,0:T(8,128)(2,1)S(1)}, u32[]{:S(2)}, u32[]{:S(2)}) collective-permute-start(bf16[1,1024,256]{2,1,0:T(8,128)(2,1)S(1)} %pad_maximum_fusion), channel_id=1, source_target_pairs={{0,2},{1,3},{2,0},{3,1},{4,6},{5,7},{6,4},{7,5},{8,10},{9,11},{10,... | collective-permute-start | bytes 1572872 | tf_op jit(solution)/shard_map/ppermute | solution.py:16
  14.7 12.0 %copy-start.3 = (bf16[1,512,256]{2,1,0:T(8,128)(2,1)S(1)}, bf16[1,512,256]{2,1,0:T(8,128)(2,1)}, u32[]{:S(2)}) copy-start(bf16[1,512,256]{2,1,0:T(8,128)(2,1)} %param.9) | copy-start | bytes 786436
  42.9 9.7 %copy-start.1 = (f32[32,16384]{1,0:T(8,128)S(1)}, f32[32,16384]{1,0:T(8,128)}, u32[]{:S(2)}) copy-start(f32[32,16384]{1,0:T(8,128)} %get-tuple-element.253) | copy-start | bytes 6291460 | tf_op jit(solution)/shard_map/while
  58.3 1.3 copy-start.2
  73.6 9.7 %copy-start.1 = (f32[32,16384]{1,0:T(8,128)S(1)}, f32[32,16384]{1,0:T(8,128)}, u32[]{:S(2)}) copy-start(f32[32,16384]{1,0:T(8,128)} %get-tuple-element.253) | copy-start | bytes 6291460 | tf_op jit(solution)/shard_map/while
  89.0 1.3 copy-start.2
  104.2 9.7 %copy-start.1 = (f32[32,16384]{1,0:T(8,128)S(1)}, f32[32,16384]{1,0:T(8,128)}, u32[]{:S(2)}) copy-start(f32[32,16384]{1,0:T(8,128)} %get-tuple-element.253) | copy-start | bytes 6291460 | tf_op jit(solution)/shard_map/while
  119.6 1.3 copy-start.2
  134.9 9.7 %copy-start.1 = (f32[32,16384]{1,0:T(8,128)S(1)}, f32[32,16384]{1,0:T(8,128)}, u32[]{:S(2)}) copy-start(f32[32,16384]{1,0:T(8,128)} %get-tuple-element.253) | copy-start | bytes 6291460 | tf_op jit(solution)/shard_map/while
  150.3 1.3 copy-start.2
  165.6 9.7 %copy-start.1 = (f32[32,16384]{1,0:T(8,128)S(1)}, f32[32,16384]{1,0:T(8,128)}, u32[]{:S(2)}) copy-start(f32[32,16384]{1,0:T(8,128)} %get-tuple-element.253) | copy-start | bytes 6291460 | tf_op jit(solution)/shard_map/while
  181.0 1.3 copy-start.2
  196.2 9.7 %copy-start.1 = (f32[32,16384]{1,0:T(8,128)S(1)}, f32[32,16384]{1,0:T(8,128)}, u32[]{:S(2)}) copy-start(f32[32,16384]{1,0:T(8,128)} %get-tuple-element.253) | copy-start | bytes 6291460 | tf_op jit(solution)/shard_map/while
  211.6 1.3 copy-start.2
  226.9 9.7 %copy-start.1 = (f32[32,16384]{1,0:T(8,128)S(1)}, f32[32,16384]{1,0:T(8,128)}, u32[]{:S(2)}) copy-start(f32[32,16384]{1,0:T(8,128)} %get-tuple-element.253) | copy-start | bytes 6291460 | tf_op jit(solution)/shard_map/while
  242.3 1.3 copy-start.2
  257.6 9.7 %copy-start.1 = (f32[32,16384]{1,0:T(8,128)S(1)}, f32[32,16384]{1,0:T(8,128)}, u32[]{:S(2)}) copy-start(f32[32,16384]{1,0:T(8,128)} %get-tuple-element.253) | copy-start | bytes 6291460 | tf_op jit(solution)/shard_map/while
  273.0 1.3 copy-start.2
  277.0 44.3 %copy-start.4 = (f32[256]{0:T(256)S(1)}, f32[256]{0:T(256)}, u32[]{:S(2)}) copy-start(f32[256]{0:T(256)} %param.15) | copy-start | bytes 3076
Sparse Core Ops, SparseCore 0:
  277.2 44.1 reduce-scatter.1
